TPU v7x, 512 devices: a whole 4x4x16 slice. The times are simulated.
512 devices in a mesh: branch: 8 (over z_lo), tok: 64 (over y, z_hi, x, core).
Axes of the slice: x: 4, y: 4, z: 16 (z_hi: 2, z_lo: 8; z = z_hi * 8 + z_lo), core: 2. Of those that a mesh axis runs over, the one named last changes fastest.
Arguments:
- teacher_hidden: bfloat16 [8, 1024, 4096], P('branch', 'tok'), may hold values from -400 to 400
- teacher_gain: float32 [8, 4096], P('branch'), may hold values from 0.5 to 1.5
- teacher_head: bfloat16 [8, 4096, 20480], P('branch', None, 'tok'), may hold values from -30 to 30
- student_hidden: bfloat16 [1024, 4096], P('branch'), may hold values from -400 to 400
- student_gain: float32 [4096], replicated, may hold values from 0.5 to 1.5
- student_head: bfloat16 [4096, 20480], P('branch', 'tok'), may hold values from -30 to 30
- cluster_weights: int32 [1024, 8], P(None, 'branch'), may hold values from 0 to 64, as said below
- token_ids: int32 [1024], P('branch'), may hold values from 0 to 20479
Outputs:
- grad_head: float32 [4096, 20480], P('branch', 'tok')
- grad_hidden: float32 [1024, 4096], P('branch', 'tok')
- grad_gain: float32 [4096], P('tok')
Inputs may be any that keep to these rules, and one draw needn't show every extreme that they name: `cluster_weights`: each token's 8 weights sum to 64.
All inputs are finite; a program needn't handle non-finite values.
Results may differ from a plain program's by a relative error of at most 0.0063.
Values may be sent and summed in bfloat16 or wider, within the bound.
A program may use at most 64 MiB of HBM per device.

v0:
```python
import jax
import jax.numpy as jnp
from jax import lax
from jax.sharding import Mesh
from jax.sharding import PartitionSpec as P

DEN = 64
TOK = ("tok_0", "tok_1", "tok_2", "tok_3")
eps = 1e-05
mix_label = 0.25
loss_scale = 64.0


def copy_for_each(value, axis):
    copies = jnp.broadcast_to(value, (lax.axis_size(axis), *value.shape))
    return lax.all_to_all(copies, axis, split_axis=0, concat_axis=0, tiled=True)


def collected_together(value, axis):
    leaves = jax.tree.leaves(value)
    turns = sorted(range(len(leaves)), key=lambda k: -leaves[k].size)
    width = (1, *leaves[turns[0]].shape)[-1]
    lines = [
        jnp.pad(leaves[k].reshape(-1), (0, -leaves[k].size % width)).reshape(-1, width)
        for k in turns
    ]
    both, at, found = (copy_for_each(jnp.concatenate(lines), axis), 0, {})
    for k, line in zip(turns, lines):
        slab = both[:, at : at + len(line)].reshape(len(both), -1)
        found[k] = slab[:, : leaves[k].size].reshape(-1, *leaves[k].shape)
        at += len(line)
    numbers = iter(range(len(leaves)))
    return jax.tree.map(lambda _: found[next(numbers)], value)


def joined_by_halves(pieces, combine):
    while len(jax.tree.leaves(pieces)[0]) > 1:
        pieces = jax.vmap(combine)(
            *(jax.tree.map(lambda part: part[side::2], pieces) for side in (0, 1))
        )
    return jax.tree.map(lambda part: part[0], pieces)


def joined_all(value, axis, combine):
    pieces = collected_together(value, axis)
    return joined_by_halves(pieces, combine)


def cut_along(value, dim, size):
    dims = value.shape
    blocks = value.reshape(*dims[:dim], size, dims[dim] // size, *dims[dim + 1 :])
    return jnp.moveaxis(blocks, dim, 0)


def summed_on_arrival(value, axis, dim):
    blocks = cut_along(value, dim, lax.axis_size(axis))
    arrived = lax.all_to_all(blocks, axis, split_axis=0, concat_axis=0, tiled=True)
    return arrived.sum(axis=0)


def in_order(blocks, dim):
    dims = list(blocks.shape[1:])
    dims[dim] *= blocks.shape[0]
    return jnp.moveaxis(blocks, 0, dim).reshape(dims)


def gathered_copies(value, axis, dim):
    blocks = copy_for_each(value, axis)
    return in_order(blocks, dim)


def summed_rows(value, axes, dim):
    far, near = axes
    blocks = cut_along(value, dim, lax.axis_size(far))
    nearer = summed_on_arrival(blocks, near, dim + 1)
    arrived = lax.all_to_all(nearer, far, split_axis=0, concat_axis=0, tiled=True)
    return arrived.sum(axis=0)


def over_copies(value, axis):
    everything = copy_for_each(value, axis)
    return jnp.sum(everything, axis=0)


def normalize(hidden, gain):
    values = hidden.astype(jnp.float32)
    inv_scale = lax.rsqrt(jnp.mean(values * values, axis=-1, keepdims=True) + eps)
    return ((values * inv_scale * gain).astype(jnp.bfloat16), inv_scale)


def combine_stats(first, second):
    top = jnp.maximum(first[0], second[0])
    return (top, first[1] * jnp.exp(first[0] - top) + second[1] * jnp.exp(second[0] - top))


def probabilities(logits):
    local_max = jnp.max(logits, axis=1)
    local_scaled = jnp.exp(logits - local_max[:, None])
    row_max, row_total = joined_all((local_max, jnp.sum(local_scaled, axis=1)), TOK, combine_stats)
    scaled = local_scaled * jnp.exp(local_max - row_max)[:, None]
    return scaled / row_total[:, None]


def per_device(
    teacher_hidden,
    teacher_gain,
    teacher_head,
    student_hidden,
    student_gain,
    student_head,
    cluster_weights,
    token_ids,
):
    width = student_hidden.shape[1]
    head_cols = teacher_head.shape[2]
    branch_gain = teacher_gain[0]
    branch_head = teacher_head[0]
    normed, unused_scale = normalize(
        lax.all_gather(teacher_hidden[0], TOK, axis=0, tiled=True), branch_gain
    )
    teacher_logits = jnp.dot(normed, branch_head, preferred_element_type=jnp.float32)
    weight = cluster_weights[:, 0].astype(jnp.float32) / DEN
    terms = probabilities(teacher_logits) * weight[:, None]
    mixed = summed_on_arrival(terms, "branch", 0)
    student_normed, inv_scale = normalize(student_hidden, student_gain)
    whole_head = gathered_copies(student_head, "branch", 0)
    student_logits = jnp.dot(student_normed, whole_head, preferred_element_type=jnp.float32)
    student_probs = probabilities(student_logits)
    offset = lax.axis_index(TOK) * head_cols
    onehot = (
        token_ids[:, None] == offset + jnp.arange(head_cols, dtype=jnp.int32)[None, :]
    ).astype(jnp.float32)
    targets = (1.0 - mix_label) * mixed + mix_label * onehot
    logit_grads = (loss_scale * (student_probs - targets)).astype(jnp.bfloat16)
    contract = (((1,), (1,)), ((), ()))
    partial_grads = lax.dot_general(
        logit_grads, whole_head, contract, preferred_element_type=jnp.float32
    )
    normed_grads = summed_rows(partial_grads, (("tok_0", "tok_1", "tok_2"), "tok_3"), 1)
    slice_width = normed_grads.shape[1]
    col_start = lax.axis_index(TOK) * slice_width
    hidden_cols = lax.dynamic_slice_in_dim(student_hidden, col_start, slice_width, 1).astype(
        jnp.float32
    )
    gain_cols = lax.dynamic_slice_in_dim(student_gain, col_start, slice_width, 0)
    grad_gain = over_copies(jnp.sum(normed_grads * hidden_cols * inv_scale, axis=0), "branch")
    row_dots = over_copies(jnp.sum(gain_cols[None, :] * normed_grads * hidden_cols, axis=1), TOK)
    grad_hidden = (
        inv_scale * gain_cols[None, :] * normed_grads
        - hidden_cols * inv_scale**3 * row_dots[:, None] / width
    )
    exchanged = lax.all_to_all(student_normed, "branch", split_axis=1, concat_axis=0, tiled=True)
    all_grads = gathered_copies(logit_grads, "branch", 0)
    grad_head = lax.dot_general(
        exchanged, all_grads, (((0,), (0,)), ((), ())), preferred_element_type=jnp.float32
    )
    return (grad_head, grad_hidden, grad_gain)


def solution(mesh):
    split = Mesh(
        mesh.devices.reshape(mesh.shape["branch"], 4, 2, 4, 2),
        ("branch", "tok_0", "tok_1", "tok_2", "tok_3"),
    )
    in_specs = (
        P("branch", TOK, None),
        P("branch", None),
        P("branch", None, TOK),
        P("branch", None),
        P(),
        P("branch", TOK),
        P(None, "branch"),
        P("branch"),
    )
    out_specs = (P("branch", TOK), P("branch", TOK), P(TOK))
    return jax.shard_map(
        per_device, mesh=split, in_specs=in_specs, out_specs=out_specs, check_vma=False
    )
```

profile of v0, /device:TPU:1, one launch (start us, length us, event | category | flops | bytes accessed | tf_op | source)
XLA Modules:
  0.0 602.1 jit_solution(17609629686330054629)
XLA Ops:
  7.2 0.0 copy-start
  7.2 0.0 all-gather.3.cloned.1.call-start
  7.2 0.7 all-gather.3.cloned.1.call-update
  7.9 2.8 broadcast_in_dim.12
  10.7 13.1 %all-to-all-start.1 = ((bf16[8,512,320]{1,2,0:T(8,128)(2,1)}), bf16[8,512,320]{1,2,0:T(8,128)(2,1)}, u32[]{:S(2)}, u32[]{:S(2)}) async-start(bf16[8,512,320]{1,2,0:T(8,128)(2,1)} %broadcast_in_dim.12), calls=%async_computation.1 | async-start | bytes 5242880 | tf_op jit(solution)/shard_map/all_to_all | solution.py:16
  23.8 2.3 copy.51
  26.1 210.6 %all-gather.3.cloned.1.call-done = bf16[1,1024,4096]{2,1,0:T(8,128)(2,1)} async-done(((bf16[1,16,4096]{2,1,0:T(8,128)(2,1)}), bf16[1,1024,4096]{2,1,0:T(8,128)(2,1)}) %all-gather.3.cloned.1.call-update) | async-done | bytes 8388624 | tf_op jit(solution)/shard_map/all_gather | solution.py:119
  236.7 5.2 fusion
  241.9 0.0 copy-done
  241.9 0.0 copy-done.7
  242.0 0.5 copy-done.2
  242.5 3.3 fusion.28
  245.7 0.0 copy-start.3
  245.8 0.0 copy-start.5
  245.8 0.0 copy-start.4
  245.8 1.0 copy-done.3
  246.8 0.2 fusion.14
  247.0 0.0 all-to-all-done.1
  247.0 0.9 broadcast_in_dim.14
  248.0 6.0 all-to-all-start.3
  253.9 1.8 fusion.11
  255.7 0.0 copy-done.5
  255.7 1.7 fusion.13
  257.5 0.0 copy-start.1
  257.5 2.4 copy.69
  259.9 0.9 fusion.29
  260.8 0.1 fusion.16
  260.9 26.4 %all-to-all-done.3 = f32[64,2,1024]{2,1,0:T(2,128)S(1)} async-done(((f32[64,2,1024]{2,1,0:T(2,128)}), f32[64,2,1024]{2,1,0:T(2,128)S(1)}, u32[]{:S(2)}, u32[]{:S(2)}) %all-to-all-start.3) | async-done | bytes 524320 | tf_op jit(solution)/shard_map/all_to_all | solution.py:16
  287.3 0.6 broadcast_in_dim.13
  288.0 7.5 %all-to-all-start.2 = ((f32[64,2,128]{2,1,0:T(2,128)}), f32[64,2,128]{2,1,0:T(2,128)S(1)}, u32[]{:S(2)}, u32[]{:S(2)}) async-start(f32[64,2,128]{2,1,0:T(2,128)} %broadcast_in_dim.13), calls=%async_computation.2 | async-start | bytes 131072 | tf_op jit(solution)/shard_map/all_to_all | solution.py:16
  295.5 0.4 fusion.26
  295.9 0.1 copy_bitcast_fusion.2
  296.1 0.7 slice.204
  296.8 1.0 multiply_add_fusion
  298.4 2.7 copy_bitcast_fusion.1
  301.1 11.2 %all-to-all-done.2 = f32[64,2,128]{2,1,0:T(2,128)S(1)} async-done(((f32[64,2,128]{2,1,0:T(2,128)}), f32[64,2,128]{2,1,0:T(2,128)S(1)}, u32[]{:S(2)}, u32[]{:S(2)}) %all-to-all-start.2) | async-done | bytes 65568 | tf_op jit(solution)/shard_map/all_to_all | solution.py:16
  312.3 13.7 %all-to-all-start.4 = ((f32[8,128,320]{1,2,0:T(8,128)}), f32[8,128,320]{1,2,0:T(8,128)}, u32[]{:S(2)}, u32[]{:S(2)}) async-start(f32[8,128,320]{1,2,0:T(8,128)} %copy_bitcast_fusion.1), calls=%async_computation.4 | async-start | bytes 2621440 | tf_op jit(solution)/shard_map/all_to_all | solution.py:57
  326.0 2.3 copy.52
  328.2 4.7 copy.53
  332.9 5.3 dot_general.17
  338.3 0.1 fusion.27
  338.8 49.2 %all-to-all-done.4 = f32[8,128,320]{1,2,0:T(8,128)} async-done(((f32[8,128,320]{1,2,0:T(8,128)}), f32[8,128,320]{1,2,0:T(8,128)}, u32[]{:S(2)}, u32[]{:S(2)}) %all-to-all-start.4) | async-done | bytes 1310752 | tf_op jit(solution)/shard_map/all_to_all | solution.py:57
  387.9 1.4 reduce_sum.103
  389.4 0.1 multiply_convert_fusion
  389.5 3.2 fusion.9
  392.7 0.2 copy.76
  392.9 7.5 %all_to_all.63 = f32[2,32,128,64]{2,3,1,0:T(8,128)} all-to-all(f32[2,32,128,64]{2,3,1,0:T(8,128)S(1)} %bitcast.68), channel_id=1, replica_groups=mesh['branch'=8,'tok_0'=4,'tok_1'=2,'tok_2'=4,'tok_3'=2] {'tok_3'}, dimensions={0} | all-to-all | bytes 4194304 | tf_op jit(solution)/shard_map/all_to_all | solution.py:57
  400.4 4.2 all-to-all-start
  404.7 2.8 reduce_sum.104
  407.5 48.0 %all-to-all-done = bf16[128,8,512]{2,0,1:T(8,128)(2,1)} async-done(((bf16[128,8,512]{2,0,1:T(8,128)(2,1)}), bf16[128,8,512]{2,0,1:T(8,128)(2,1)}, u32[]{:S(2)}, u32[]{:S(2)}) %all-to-all-start) | async-done | bytes 1048608 | tf_op jit(solution)/shard_map/all_to_all | solution.py:152
  455.5 51.6 %all_to_all.64 = f32[32,128,64]{1,2,0:T(8,128)} all-to-all(f32[32,128,64]{1,2,0:T(8,128)} %reduce_sum.104), channel_id=1, replica_groups=mesh['branch'=8,'tok_0'=4,'tok_1'=2,'tok_2'=4,'tok_3'=2] {'tok_0','tok_1..., dimensions={0} | all-to-all | bytes 2097152 | tf_op jit(solution)/shard_map/all_to_all | solution.py:76
  507.0 0.9 broadcast_in_dim.15
  507.9 14.0 %all-to-all-start.5 = ((bf16[8,128,320]{1,2,0:T(8,128)(2,1)}), bf16[8,128,320]{1,2,0:T(8,128)(2,1)S(1)}, u32[]{:S(2)}, u32[]{:S(2)}) async-start(bf16[8,128,320]{1,2,0:T(8,128)(2,1)} %broadcast_in_dim.15), calls=%async_computation.5 | async-start | bytes 1310720 | tf_op jit(solution)/shard_map/all_to_all | solution.py:16
  521.9 0.1 dynamic_slice.6
  522.0 1.3 reduce_sum.105
  523.3 0.9 fusion.23
  524.2 21.7 %all-to-all-done.5 = bf16[8,128,320]{1,2,0:T(8,128)(2,1)S(1)} async-done(((bf16[8,128,320]{1,2,0:T(8,128)(2,1)}), bf16[8,128,320]{1,2,0:T(8,128)(2,1)S(1)}, u32[]{:S(2)}, u32[]{:S(2)}) %all-to-all-start.5) | async-done | bytes 655392 | tf_op jit(solution)/shard_map/all_to_all | solution.py:16
  546.0 22.7 %all_to_all.65 = f32[8,1,64]{2,1,0:T(1,128)S(1)} all-to-all(f32[8,1,64]{2,1,0:T(1,128)S(1)} %broadcast_in_dim.17), channel_id=1, replica_groups=mesh['branch'=8,'tok_0'=4,'tok_1'=2,'tok_2'=4,'tok_3'=2] {'branch'}, dimensions={0} | all-to-all | bytes 4096 | tf_op jit(solution)/shard_map/all_to_all | solution.py:16
  568.6 0.6 broadcast_in_dim.16
  569.3 8.1 %all-to-all-start.8 = ((f32[64,1,128]{2,1,0:T(1,128)}), f32[64,1,128]{2,1,0:T(1,128)S(1)}, u32[]{:S(2)}, u32[]{:S(2)}) async-start(f32[64,1,128]{2,1,0:T(1,128)} %broadcast_in_dim.16), calls=%async_computation.8 | async-start | bytes 65536 | tf_op jit(solution)/shard_map/all_to_all | solution.py:16
  577.4 2.6 convolution_bitcast_fusion
  580.0 0.5 reduce_sum.109
  580.5 13.3 %all-to-all-done.8 = f32[64,1,128]{2,1,0:T(1,128)S(1)} async-done(((f32[64,1,128]{2,1,0:T(1,128)}), f32[64,1,128]{2,1,0:T(1,128)S(1)}, u32[]{:S(2)}, u32[]{:S(2)}) %all-to-all-start.8) | async-done | bytes 32800 | tf_op jit(solution)/shard_map/all_to_all | solution.py:16
  593.8 1.4 fusion.20
  (66 shorter events, 1.1 us)
Async XLA Ops:
  7.2 234.8 %copy-start = (bf16[1,4096,320]{1,2,0:T(8,128)(2,1)S(1)}, bf16[1,4096,320]{1,2,0:T(8,128)(2,1)}, u32[]{:S(2)}) copy-start(bf16[1,4096,320]{1,2,0:T(8,128)(2,1)} %param.10) | copy-start | bytes 7864324
  7.2 229.5 %all-gather.3.cloned.1.call-start = ((), (), s32[]{:S(2)}) async-start(), calls=%async_computation.10 | async-start | bytes 8519680 | tf_op jit(solution)/shard_map/all_gather | solution.py:119
  10.7 236.3 %all-to-all-start.1 = ((bf16[8,512,320]{1,2,0:T(8,128)(2,1)}), bf16[8,512,320]{1,2,0:T(8,128)(2,1)}, u32[]{:S(2)}, u32[]{:S(2)}) async-start(bf16[8,512,320]{1,2,0:T(8,128)(2,1)} %broadcast_in_dim.12), calls=%async_computation.1 | async-start | bytes 5242880 | tf_op jit(solution)/shard_map/all_to_all | solution.py:16
  23.8 218.1 %copy-start.7 = (f32[1,4096]{1,0:T(1,128)S(1)}, f32[1,4096]{1,0:T(1,128)}, u32[]{:S(2)}) copy-start(f32[1,4096]{1,0:T(1,128)} %param.9) | copy-start | bytes 49156
  236.7 5.8 copy-start.2
  245.7 1.0 copy-start.3
  245.8 10.0 %copy-start.5 = (s32[1024,1]{0,1:T(1,128)S(1)}, s32[1024,1]{0,1:T(1,128)}, u32[]{:S(2)}) copy-start(s32[1024,1]{0,1:T(1,128)} %param.14) | copy-start | bytes 12292
  245.8 10.0 %copy-start.4 = (f32[4096]{0:T(1024)S(1)}, f32[4096]{0:T(1024)}, u32[]{:S(2)}) copy-start(f32[4096]{0:T(1024)} %param.12) | copy-start | bytes 49156
  248.0 39.4 %all-to-all-start.3 = ((f32[64,2,1024]{2,1,0:T(2,128)}), f32[64,2,1024]{2,1,0:T(2,128)S(1)}, u32[]{:S(2)}, u32[]{:S(2)}) async-start(f32[64,2,1024]{2,1,0:T(2,128)} %broadcast_in_dim.14), calls=%async_computation.3 | async-start | bytes 1048576 | tf_op jit(solution)/shard_map/all_to_all | solution.py:16
  257.5 2.4 copy-start.1
  288.0 24.3 %all-to-all-start.2 = ((f32[64,2,128]{2,1,0:T(2,128)}), f32[64,2,128]{2,1,0:T(2,128)S(1)}, u32[]{:S(2)}, u32[]{:S(2)}) async-start(f32[64,2,128]{2,1,0:T(2,128)} %broadcast_in_dim.13), calls=%async_computation.2 | async-start | bytes 131072 | tf_op jit(solution)/shard_map/all_to_all | solution.py:16
  312.3 75.7 %all-to-all-start.4 = ((f32[8,128,320]{1,2,0:T(8,128)}), f32[8,128,320]{1,2,0:T(8,128)}, u32[]{:S(2)}, u32[]{:S(2)}) async-start(f32[8,128,320]{1,2,0:T(8,128)} %copy_bitcast_fusion.1), calls=%async_computation.4 | async-start | bytes 2621440 | tf_op jit(solution)/shard_map/all_to_all | solution.py:57
  332.9 56.4 %copy-start.6 = (s32[128]{0:T(128)S(1)}, s32[128]{0:T(128)}, u32[]{:S(2)}) copy-start(s32[128]{0:T(128)} %param.15) | copy-start | bytes 1540
  400.4 55.1 %all-to-all-start = ((bf16[128,8,512]{2,0,1:T(8,128)(2,1)}), bf16[128,8,512]{2,0,1:T(8,128)(2,1)}, u32[]{:S(2)}, u32[]{:S(2)}) async-start(bf16[128,8,512]{2,0,1:T(8,128)(2,1)} %copy.52), calls=%async_computation | async-start | bytes 2097152 | tf_op jit(solution)/shard_map/all_to_all | solution.py:152
  507.9 38.0 %all-to-all-start.5 = ((bf16[8,128,320]{1,2,0:T(8,128)(2,1)}), bf16[8,128,320]{1,2,0:T(8,128)(2,1)S(1)}, u32[]{:S(2)}, u32[]{:S(2)}) async-start(bf16[8,128,320]{1,2,0:T(8,128)(2,1)} %broadcast_in_dim.15), calls=%async_computation.5 | async-start | bytes 1310720 | tf_op jit(solution)/shard_map/all_to_all | solution.py:16
  569.3 24.6 %all-to-all-start.8 = ((f32[64,1,128]{2,1,0:T(1,128)}), f32[64,1,128]{2,1,0:T(1,128)S(1)}, u32[]{:S(2)}, u32[]{:S(2)}) async-start(f32[64,1,128]{2,1,0:T(1,128)} %broadcast_in_dim.16), calls=%async_computation.8 | async-start | bytes 65536 | tf_op jit(solution)/shard_map/all_to_all | solution.py:16
Sparse Core Ops, SparseCore 0:
  12.6 224.0 all-gather.2
where the time goes:
time: 603 us; the launch traced here: 602 us
  waiting for transfers between devices  381 us (63%)
  blocking collectives  81.7 us (14%)
  starting transfers between devices  66.6 us (11%)
  local copies, waits for them, and re-layouts  26.8 us (4%)
  other arithmetic  21.5 us (4%)
  between operations  14.4 us (2%)
  matrix products  9.89 us (2%)
    all_gather x1, waiting for transfers between devices, per_device(): lax.all_gather(teacher_hidden[0], TOK, axis=0, tiled=True)  211 us
    all_to_all x5, waiting for transfers between devices, copy_for_each(): return lax.all_to_all(copies, axis, split_axis=0, concat_axis=0, tiled=True)  72.7 us
    all_to_all x1, blocking collectives, summed_rows(): lax.all_to_all(nearer, far, split_axis=0, concat_axis=0, tiled=True)  51.6 us
    all_to_all x1, waiting for transfers between devices, summed_on_arrival(): lax.all_to_all(blocks, axis, split_axis=0, concat_axis=0, tiled=True)  49.2 us
    all_to_all x5, starting transfers between devices, copy_for_each(): return lax.all_to_all(copies, axis, split_axis=0, concat_axis=0, tiled=True)  48.7 us
    all_to_all x1, waiting for transfers between devices, per_device(): lax.all_to_all(student_normed, 'branch', split_axis=1, concat_axis=0, til...  48 us
    all_to_all x1, blocking collectives, copy_for_each(): return lax.all_to_all(copies, axis, split_axis=0, concat_axis=0, tiled=True)  22.7 us
    all_to_all x1, starting transfers between devices, summed_on_arrival(): lax.all_to_all(blocks, axis, split_axis=0, concat_axis=0, tiled=True)  13.7 us
  transfers between devices with their start and end apart: 8, of which 7 were waited for; matrix products, arithmetic and copies ran while one was open for 8% of the time, Pallas kernels for 0%

commit v1 on v0

--- a/solution.py
+++ b/solution.py
@@ -115,9 +115,16 @@
     head_cols = teacher_head.shape[2]
     branch_gain = teacher_gain[0]
     branch_head = teacher_head[0]
-    normed, unused_scale = normalize(
-        lax.all_gather(teacher_hidden[0], TOK, axis=0, tiled=True), branch_gain
+    load_the_indices = lambda which_axis, frame_in: jnp.concatenate(
+        lax.all_to_all(
+            jnp.stack([frame_in] * lax.axis_size(which_axis)),
+            split_axis=0,
+            axis_name=which_axis,
+            concat_axis=0,
+        ),
+        0,
     )
+    normed, unused_scale = normalize(load_the_indices(TOK, teacher_hidden[0]), branch_gain)
     teacher_logits = jnp.dot(normed, branch_head, preferred_element_type=jnp.float32)
     weight = cluster_weights[:, 0].astype(jnp.float32) / DEN
     terms = probabilities(teacher_logits) * weight[:, None]

time: 603 us -> 867 us (1.44)
  blocking collectives: 81.7 us -> 365 us
  waiting for transfers between devices: 381 us -> 256 us
  starting transfers between devices: 66.6 us -> 173 us
  between operations: 14.4 us -> 1.04 us
  other arithmetic: 21.5 us -> 31.7 us
    all_to_all x0 -> x1, blocking collectives: none -> 283 us  [per_device(): lax.all_to_all(jnp.stack([frame_in] * lax.axis_size(which_axis)), split_a...]
    all_gather x1 -> x0, waiting for transfers between devices: 211 us -> none  [per_device(): lax.all_gather(teacher_hidden[0], TOK, axis=0, tiled=True)]
    all_to_all x5, starting transfers between devices: 48.7 us -> 162 us  [copy_for_each(): return lax.all_to_all(copies, axis, split_axis=0, concat_axis=0, tiled=True)]
    all_to_all x5, waiting for transfers between devices: 72.7 us -> 159 us  [copy_for_each(): return lax.all_to_all(copies, axis, split_axis=0, concat_axis=0, tiled=True)]
    convert_element_type x1 -> x2, other arithmetic: 1.75 us -> 12.1 us  [normalize(): return ((values * inv_scale * gain).astype(jnp.bfloat16), inv_scale)]
  transfers between devices with their start and end apart: 8 -> 7, of which waited for: 7 -> 7; matrix products, arithmetic and copies ran while one was open for 8% -> 7% of each run, Pallas kernels for 0% -> 0%
where the time goes in v1:
time: 867 us; the launch traced here: 866 us
  blocking collectives  365 us (42%)
  waiting for transfers between devices  256 us (30%)
  starting transfers between devices  173 us (20%)
  other arithmetic  31.7 us (4%)
  local copies, waits for them, and re-layouts  27.4 us (3%)
  matrix products  12 us (1%)
    all_to_all x1, blocking collectives, per_device(): lax.all_to_all(jnp.stack([frame_in] * lax.axis_size(which_axis)), split_a...  283 us
    all_to_all x5, starting transfers between devices, copy_for_each(): return lax.all_to_all(copies, axis, split_axis=0, concat_axis=0, tiled=True)  162 us
    all_to_all x5, waiting for transfers between devices, copy_for_each(): return lax.all_to_all(copies, axis, split_axis=0, concat_axis=0, tiled=True)  159 us
    all_to_all x1, blocking collectives, summed_rows(): lax.all_to_all(nearer, far, split_axis=0, concat_axis=0, tiled=True)  51.5 us
    all_to_all x1, waiting for transfers between devices, summed_on_arrival(): lax.all_to_all(blocks, axis, split_axis=0, concat_axis=0, tiled=True)  49.2 us
    all_to_all x1, waiting for transfers between devices, per_device(): lax.all_to_all(student_normed, 'branch', split_axis=1, concat_axis=0, til...  48 us
    all_to_all x1, blocking collectives, copy_for_each(): return lax.all_to_all(copies, axis, split_axis=0, concat_axis=0, tiled=True)  22.7 us
  transfers between devices with their start and end apart: 7, of which 7 were waited for; matrix products, arithmetic and copies ran while one was open for 7% of the time, Pallas kernels for 0%

profile of v1, /device:TPU:1, one launch (start us, length us, event | category | flops | bytes accessed | tf_op | source)
XLA Modules:
  0.0 865.9 jit_solution(3232462583433828311)
XLA Ops:
  0.6 0.0 copy-start
  0.6 2.1 stack.3
  2.7 0.0 copy-start.3
  2.8 283.2 %all_to_all.68 = bf16[64,16,4096]{2,1,0:T(8,128)(2,1)} all-to-all(bf16[64,16,4096]{2,1,0:T(8,128)(2,1)S(1)} %stack.3), channel_id=1, replica_groups=mesh['branch'=8,'tok_0'=4,'tok_1'=2,'tok_2'=4,'tok_3'=2] {'tok_0','tok_1..., dimensions={0} | all-to-all | bytes 16777216 | tf_op jit(solution)/shard_map/all_to_all | solution.py:119
  286.0 1.8 broadcast_in_dim.12
  287.8 118.8 %all-to-all-start.1 = ((bf16[8,512,320]{1,2,0:T(8,128)(2,1)}), bf16[8,512,320]{1,2,0:T(8,128)(2,1)}, u32[]{:S(2)}, u32[]{:S(2)}) async-start(bf16[8,512,320]{1,2,0:T(8,128)(2,1)} %broadcast_in_dim.12), calls=%async_computation.1 | async-start | bytes 5242880 | tf_op jit(solution)/shard_map/all_to_all | solution.py:16
  406.6 2.3 copy.51
  408.9 5.1 fusion
  414.0 0.0 copy-done.4
  414.0 10.3 %fusion.2 = bf16[64,16,4096]{2,1,0:T(8,128)(2,1)} fusion(bf16[64,16,4096]{2,1,0:T(8,128)(2,1)} %all_to_all.68, f32[4096]{0:T(1024)S(1)} %bitcast.71, f32[64,16]{1,0:T(8,128)S(1)} %add_rsqrt_fusion), kind=kLoop, calls=%fused_computation.4 | loop fusion | flops 16777216 | bytes 16797696 | tf_op jit(solution)/shard_map/convert_element_type | solution.py:88
  424.3 0.0 copy-done
  424.3 5.3 fusion.24
  429.7 0.0 copy-start.2
  429.7 0.0 copy-start.6
  429.7 0.0 copy-start.5
  429.7 1.0 copy-done.2
  430.8 0.2 fusion.10
  431.0 94.1 %all-to-all-done.1 = bf16[8,512,320]{1,2,0:T(8,128)(2,1)} async-done(((bf16[8,512,320]{1,2,0:T(8,128)(2,1)}), bf16[8,512,320]{1,2,0:T(8,128)(2,1)}, u32[]{:S(2)}, u32[]{:S(2)}) %all-to-all-start.1) | async-done | bytes 2621472 | tf_op jit(solution)/shard_map/all_to_all | solution.py:16
  525.1 0.9 broadcast_in_dim.14
  526.0 6.6 all-to-all-start.4
  532.6 1.8 fusion.7
  534.5 1.7 fusion.9
  536.2 0.0 copy-start.1
  536.2 2.4 copy.69
  538.6 0.0 copy-done.1
  538.7 0.9 fusion.25
  539.5 0.1 fusion.12
  539.6 18.3 %all-to-all-done.4 = f32[64,2,1024]{2,1,0:T(2,128)S(1)} async-done(((f32[64,2,1024]{2,1,0:T(2,128)}), f32[64,2,1024]{2,1,0:T(2,128)S(1)}, u32[]{:S(2)}, u32[]{:S(2)}) %all-to-all-start.4) | async-done | bytes 524320 | tf_op jit(solution)/shard_map/all_to_all | solution.py:16
  557.9 0.6 broadcast_in_dim.13
  558.6 14.0 %all-to-all-start.2 = ((f32[64,2,128]{2,1,0:T(2,128)}), f32[64,2,128]{2,1,0:T(2,128)S(1)}, u32[]{:S(2)}, u32[]{:S(2)}) async-start(f32[64,2,128]{2,1,0:T(2,128)} %broadcast_in_dim.13), calls=%async_computation.2 | async-start | bytes 131072 | tf_op jit(solution)/shard_map/all_to_all | solution.py:16
  572.5 0.4 fusion.22
  572.9 0.1 copy_bitcast_fusion.2
  573.1 0.7 slice.204
  573.9 1.0 multiply_add_fusion
  575.4 2.7 copy_bitcast_fusion.1
  578.1 11.2 %all-to-all-done.2 = f32[64,2,128]{2,1,0:T(2,128)S(1)} async-done(((f32[64,2,128]{2,1,0:T(2,128)}), f32[64,2,128]{2,1,0:T(2,128)S(1)}, u32[]{:S(2)}, u32[]{:S(2)}) %all-to-all-start.2) | async-done | bytes 65568 | tf_op jit(solution)/shard_map/all_to_all | solution.py:16
  589.3 7.3 all-to-all-start.5
  596.6 2.2 copy.52
  598.9 4.7 copy.53
  603.6 5.3 dot_general.17
  608.9 0.1 fusion.23
  609.4 49.2 %all-to-all-done.5 = f32[8,128,320]{1,2,0:T(8,128)} async-done(((f32[8,128,320]{1,2,0:T(8,128)}), f32[8,128,320]{1,2,0:T(8,128)}, u32[]{:S(2)}, u32[]{:S(2)}) %all-to-all-start.5) | async-done | bytes 1310752 | tf_op jit(solution)/shard_map/all_to_all | solution.py:57
  658.6 1.4 reduce_sum.103
  660.0 0.1 multiply_convert_fusion
  660.1 3.2 fusion.5
  663.4 0.2 copy.76
  663.6 7.5 all_to_all.69
  671.1 4.2 all-to-all-start
  675.3 2.8 reduce_sum.104
  678.2 48.0 %all-to-all-done = bf16[128,8,512]{2,0,1:T(8,128)(2,1)} async-done(((bf16[128,8,512]{2,0,1:T(8,128)(2,1)}), bf16[128,8,512]{2,0,1:T(8,128)(2,1)}, u32[]{:S(2)}, u32[]{:S(2)}) %all-to-all-start) | async-done | bytes 1048608 | tf_op jit(solution)/shard_map/all_to_all | solution.py:159
  726.1 51.5 %all_to_all.70 = f32[32,128,64]{1,2,0:T(8,128)} all-to-all(f32[32,128,64]{1,2,0:T(8,128)} %reduce_sum.104), channel_id=1, replica_groups=mesh['branch'=8,'tok_0'=4,'tok_1'=2,'tok_2'=4,'tok_3'=2] {'tok_0','tok_1..., dimensions={0} | all-to-all | bytes 2097152 | tf_op jit(solution)/shard_map/all_to_all | solution.py:76
  777.6 0.9 broadcast_in_dim.15
  778.6 14.0 %all-to-all-start.6 = ((bf16[8,128,320]{1,2,0:T(8,128)(2,1)}), bf16[8,128,320]{1,2,0:T(8,128)(2,1)S(1)}, u32[]{:S(2)}, u32[]{:S(2)}) async-start(bf16[8,128,320]{1,2,0:T(8,128)(2,1)} %broadcast_in_dim.15), calls=%async_computation.6 | async-start | bytes 1310720 | tf_op jit(solution)/shard_map/all_to_all | solution.py:16
  792.6 0.1 dynamic_slice.6
  792.7 1.3 reduce_sum.105
  794.0 0.9 fusion.19
  794.9 21.7 %all-to-all-done.6 = bf16[8,128,320]{1,2,0:T(8,128)(2,1)S(1)} async-done(((bf16[8,128,320]{1,2,0:T(8,128)(2,1)}), bf16[8,128,320]{1,2,0:T(8,128)(2,1)S(1)}, u32[]{:S(2)}, u32[]{:S(2)}) %all-to-all-start.6) | async-done | bytes 655392 | tf_op jit(solution)/shard_map/all_to_all | solution.py:16
  816.6 22.7 %all_to_all.71 = f32[8,1,64]{2,1,0:T(1,128)S(1)} all-to-all(f32[8,1,64]{2,1,0:T(1,128)S(1)} %broadcast_in_dim.17), channel_id=1, replica_groups=mesh['branch'=8,'tok_0'=4,'tok_1'=2,'tok_2'=4,'tok_3'=2] {'branch'}, dimensions={0} | all-to-all | bytes 4096 | tf_op jit(solution)/shard_map/all_to_all | solution.py:16
  839.3 0.6 broadcast_in_dim.16
  839.9 8.1 all-to-all-start.9
  848.1 2.6 convolution_bitcast_fusion
  850.6 0.5 reduce_sum.109
  851.1 13.3 %all-to-all-done.9 = f32[64,1,128]{2,1,0:T(1,128)S(1)} async-done(((f32[64,1,128]{2,1,0:T(1,128)}), f32[64,1,128]{2,1,0:T(1,128)S(1)}, u32[]{:S(2)}, u32[]{:S(2)}) %all-to-all-start.9) | async-done | bytes 32800 | tf_op jit(solution)/shard_map/all_to_all | solution.py:16
  864.5 1.4 fusion.16
  (66 shorter events, 1.1 us)
Async XLA Ops:
  0.6 423.7 %copy-start = (bf16[1,4096,320]{1,2,0:T(8,128)(2,1)S(1)}, bf16[1,4096,320]{1,2,0:T(8,128)(2,1)}, u32[]{:S(2)}) copy-start(bf16[1,4096,320]{1,2,0:T(8,128)(2,1)} %param.10) | copy-start | bytes 7864324
  2.7 283.2 %copy-start.3 = (bf16[512,320]{0,1:T(8,128)(2,1)S(1)}, bf16[512,320]{0,1:T(8,128)(2,1)}, u32[]{:S(2)}) copy-start(bf16[512,320]{0,1:T(8,128)(2,1)} %param.13) | copy-start | bytes 983044
  287.8 237.3 %all-to-all-start.1 = ((bf16[8,512,320]{1,2,0:T(8,128)(2,1)}), bf16[8,512,320]{1,2,0:T(8,128)(2,1)}, u32[]{:S(2)}, u32[]{:S(2)}) async-start(bf16[8,512,320]{1,2,0:T(8,128)(2,1)} %broadcast_in_dim.12), calls=%async_computation.1 | async-start | bytes 5242880 | tf_op jit(solution)/shard_map/all_to_all | solution.py:16
  408.9 5.1 copy-start.4
  429.7 1.1 copy-start.2
  429.7 104.7 %copy-start.6 = (s32[1024,1]{0,1:T(1,128)S(1)}, s32[1024,1]{0,1:T(1,128)}, u32[]{:S(2)}) copy-start(s32[1024,1]{0,1:T(1,128)} %param.14) | copy-start | bytes 12292
  429.7 104.7 %copy-start.5 = (f32[4096]{0:T(1024)S(1)}, f32[4096]{0:T(1024)}, u32[]{:S(2)}) copy-start(f32[4096]{0:T(1024)} %param.12) | copy-start | bytes 49156
  526.0 31.9 %all-to-all-start.4 = ((f32[64,2,1024]{2,1,0:T(2,128)}), f32[64,2,1024]{2,1,0:T(2,128)S(1)}, u32[]{:S(2)}, u32[]{:S(2)}) async-start(f32[64,2,1024]{2,1,0:T(2,128)} %broadcast_in_dim.14), calls=%async_computation.4 | async-start | bytes 1048576 | tf_op jit(solution)/shard_map/all_to_all | solution.py:16
  536.2 2.4 copy-start.1
  558.6 30.8 %all-to-all-start.2 = ((f32[64,2,128]{2,1,0:T(2,128)}), f32[64,2,128]{2,1,0:T(2,128)S(1)}, u32[]{:S(2)}, u32[]{:S(2)}) async-start(f32[64,2,128]{2,1,0:T(2,128)} %broadcast_in_dim.13), calls=%async_computation.2 | async-start | bytes 131072 | tf_op jit(solution)/shard_map/all_to_all | solution.py:16
  589.3 69.3 %all-to-all-start.5 = ((f32[8,128,320]{1,2,0:T(8,128)}), f32[8,128,320]{1,2,0:T(8,128)}, u32[]{:S(2)}, u32[]{:S(2)}) async-start(f32[8,128,320]{1,2,0:T(8,128)} %copy_bitcast_fusion.1), calls=%async_computation.5 | async-start | bytes 2621440 | tf_op jit(solution)/shard_map/all_to_all | solution.py:57
  603.6 56.4 %copy-start.7 = (s32[128]{0:T(128)S(1)}, s32[128]{0:T(128)}, u32[]{:S(2)}) copy-start(s32[128]{0:T(128)} %param.15) | copy-start | bytes 1540
  671.1 55.1 %all-to-all-start = ((bf16[128,8,512]{2,0,1:T(8,128)(2,1)}), bf16[128,8,512]{2,0,1:T(8,128)(2,1)}, u32[]{:S(2)}, u32[]{:S(2)}) async-start(bf16[128,8,512]{2,0,1:T(8,128)(2,1)} %copy.52), calls=%async_computation | async-start | bytes 2097152 | tf_op jit(solution)/shard_map/all_to_all | solution.py:159
  778.6 38.1 %all-to-all-start.6 = ((bf16[8,128,320]{1,2,0:T(8,128)(2,1)}), bf16[8,128,320]{1,2,0:T(8,128)(2,1)S(1)}, u32[]{:S(2)}, u32[]{:S(2)}) async-start(bf16[8,128,320]{1,2,0:T(8,128)(2,1)} %broadcast_in_dim.15), calls=%async_computation.6 | async-start | bytes 1310720 | tf_op jit(solution)/shard_map/all_to_all | solution.py:16
  839.9 24.6 %all-to-all-start.9 = ((f32[64,1,128]{2,1,0:T(1,128)}), f32[64,1,128]{2,1,0:T(1,128)S(1)}, u32[]{:S(2)}, u32[]{:S(2)}) async-start(f32[64,1,128]{2,1,0:T(1,128)} %broadcast_in_dim.16), calls=%async_computation.9 | async-start | bytes 65536 | tf_op jit(solution)/shard_map/all_to_all | solution.py:16
